TPU v7x, 32 devices: a whole 2x2x4 slice. The times are simulated.
32 devices in a mesh: dp: 4 (over y, x), tm: 8 (over z, core).
Axes of the slice: x: 2, y: 2, z: 4, core: 2. Of those that a mesh axis runs over, the one named last changes fastest.
Arguments:
- activations: bfloat16 [4, 16, 64, 16, 128], P('dp', 'tm')
- conv_weight: bfloat16 [3, 3, 3, 128, 128], replicated, may hold values from -0.109375 to 0.109375
- norm_gain: float32 [128], replicated, may hold values from 0.5 to 1.5
- norm_bias: float32 [128], replicated, may hold values from -0.5 to 0.5
- down_weight: bfloat16 [3, 3, 128, 128], replicated, may hold values from -0.1875 to 0.1875
- cotangent: bfloat16 [4, 16, 32, 8, 128], P('dp', None, 'tm'), may hold values from -0.625 to 0.625
Outputs:
- encoded: bfloat16 [4, 16, 32, 8, 128], P('dp', None, 'tm')
- grad_down: float32 [3, 3, 128, 128], P(None, None, None, 'tm')
All inputs are finite; a program needn't handle non-finite values.
Results may differ from a plain program's by a relative error of at most 0.005.
Values may be sent and summed in bfloat16 or wider, within the bound.
No kernel may reach another device: no remote copies, remote signals or barrier semaphores. Data moves between devices by JAX's collectives and lax.ppermute only.
A program may use at most 64 MiB of HBM per device.

v0:
```python
import jax
import jax.numpy as jnp
from jax import lax
from jax.sharding import PartitionSpec as P

G = 32


def passed_along(shard, axis, by):
    count = lax.axis_size(axis)
    pairs = [(i, i + by) for i in range(count) if 0 <= i + by < count]
    return lax.ppermute(shard, axis, pairs)


def down_patches(extended, rows_out, cols_out):
    tap_list = []
    for row_tap in range(3):
        for col_tap in range(3):
            tap_list.append(
                extended[
                    :,
                    :,
                    row_tap : row_tap + 2 * rows_out - 1 : 2,
                    col_tap : col_tap + 2 * cols_out - 1 : 2,
                    :,
                ]
            )
    return jnp.concatenate(tap_list, axis=-1)


def per_device(activations, conv_weight, norm_gain, norm_bias, down_weight, cotangent):
    clip_count, frames_dev, height, width_cells, channels = activations.shape
    out_channels = conv_weight.shape[-1]
    groups = G
    earlier = passed_along(activations, "tm", 1)
    framed = jnp.concatenate([earlier, activations], axis=1)
    framed = jnp.pad(framed, ((0, 0), (0, 0), (1, 1), (1, 1), (0, 0)))
    conv_out = jnp.zeros(
        (clip_count * frames_dev * height * width_cells, out_channels), jnp.float32
    )
    for row_tap in range(3):
        for col_tap in range(3):
            window_slab = framed[
                :, :, row_tap : row_tap + height, col_tap : col_tap + width_cells, :
            ]
            stacked = jnp.concatenate(
                [window_slab[:, time_tap : time_tap + frames_dev] for time_tap in range(3)], axis=-1
            )
            tap_weight = conv_weight[:, row_tap, col_tap].reshape(3 * channels, out_channels)
            conv_out = conv_out + jnp.dot(
                stacked.reshape(-1, 3 * channels), tap_weight, preferred_element_type=jnp.float32
            )
    grouped = conv_out.reshape(
        clip_count, frames_dev, height, width_cells, groups, channels // groups
    )
    group_sums = jnp.sum(grouped, axis=(1, 2, 3, 5))
    group_squares = jnp.sum(grouped * grouped, axis=(1, 2, 3, 5))
    group_sums, group_squares = lax.psum((group_sums, group_squares), "tm")
    members = float(frames_dev * lax.axis_size("tm") * height * width_cells * (channels // groups))
    group_mean = group_sums / members
    variance = group_squares / members - group_mean * group_mean
    inverse = lax.rsqrt(variance + 1e-06)
    normed = (
        (grouped - group_mean[:, None, None, None, :, None]) * inverse[:, None, None, None, :, None]
    ).reshape(clip_count, frames_dev, height, width_cells, channels) * norm_gain + norm_bias
    hidden = jax.nn.silu(normed).astype(jnp.bfloat16)
    down_flat = down_weight.reshape(9 * channels, -1)
    extended = jnp.pad(hidden, ((0, 0), (0, 0), (0, 1), (0, 1), (0, 0)))
    patches = down_patches(extended, height // 2, width_cells // 2)
    local_out = jnp.dot(
        patches.reshape(-1, 9 * channels), down_flat, preferred_element_type=jnp.float32
    )
    local_out = local_out.reshape(clip_count, frames_dev, height // 2, width_cells // 2, -1).astype(
        jnp.bfloat16
    )
    encoded = lax.all_to_all(local_out, "tm", split_axis=2, concat_axis=1, tiled=True)
    grad_rows = lax.all_to_all(cotangent, "tm", split_axis=1, concat_axis=2, tiled=True)
    partial_value = lax.dot_general(
        patches.reshape(-1, 9 * channels),
        grad_rows.reshape(-1, grad_rows.shape[-1]),
        (((0,), (0,)), ((), ())),
        preferred_element_type=jnp.float32,
    )
    partial_value = partial_value.reshape(3, 3, channels, -1)
    shares = lax.psum_scatter(partial_value, "tm", scatter_dimension=3, tiled=True)
    grad_down = lax.psum(shares, "dp")
    return (encoded, grad_down)


def solution(mesh):
    placed = (P("dp", "tm", None, None, None), P(), P(), P(), P(), P("dp", None, "tm", None, None))
    return jax.shard_map(
        per_device,
        mesh=mesh,
        in_specs=placed,
        out_specs=(P("dp", None, "tm", None, None), P(None, None, None, "tm")),
        check_vma=False,
    )
```

profile of v0, /device:TPU:0, one launch (start us, length us, event | category | flops | bytes accessed | tf_op | source)
XLA Modules:
  0.0 149.7 jit_solution(5531830060840235410)
XLA Ops:
  7.2 2.5 %collective-permute-start = (bf16[1,2,64,16,128]{4,3,2,1,0:T(8,128)(2,1)}, bf16[1,2,64,16,128]{4,3,2,1,0:T(8,128)(2,1)S(1)}, u32[]{:S(2)}, u32[]{:S(2)}) collective-permute-start(bf16[1,2,64,16,128]{4,3,2,1,0:T(8,128)(2,1)} %param.6), channel_id=1, source_target_pairs={{0,1},{1,2},{2,3},{3,4},{4,5},{5,6},{6,7},{8,9},{9,10},{10,11},{11... | collective-permute-start | bytes 1572872 | tf_op jit(solution)/shard_map/ppermute | solution.py:12
  9.7 6.1 %all-to-all-start.1 = ((bf16[1,16,4,8,128]{4,3,2,0,1:T(8,128)(2,1)}), bf16[1,16,4,8,128]{4,3,2,0,1:T(8,128)(2,1)S(1)}, u32[]{:S(2)}, u32[]{:S(2)}) async-start(bf16[1,16,4,8,128]{4,3,2,0,1:T(8,128)(2,1)} %bitcast.100), calls=%async_computation.1 | async-start | bytes 262144 | tf_op jit(solution)/shard_map/all_to_all | solution.py:77
  15.9 1.4 fusion.9
  17.3 5.4 %all-to-all-done.1 = bf16[1,16,4,8,128]{4,3,2,0,1:T(8,128)(2,1)S(1)} async-done(((bf16[1,16,4,8,128]{4,3,2,0,1:T(8,128)(2,1)}), bf16[1,16,4,8,128]{4,3,2,0,1:T(8,128)(2,1)S(1)}, u32[]{:S(2)}, u32[]{:S(2)}) %all-to-all-start.1) | async-done | bytes 131104 | tf_op jit(solution)/shard_map/all_to_all | solution.py:77
  22.8 3.1 %pad_slice_fusion.2 = (bf16[1,2,64,16,128]{4,3,2,1,0:T(8,128)(2,1)S(1)}, bf16[1,2,64,16,128]{4,3,2,1,0:T(8,128)(2,1)S(1)}, bf16[1,2,64,16,128]{4,3,2,1,0:T(8,128...) fusion(bf16[1,4,64,16,128]{4,3,2,1,0:T(8,128)(2,1)S(1)} %consta, ...), kind=kLoop, calls=%fused_computation.2 | loop fusion | bytes 11010048 | tf_op jit(solution)/shard_map/slice | solution.py:47
  25.9 0.6 pad_slice_fusion.1
  26.5 0.5 pad_maximum_fusion
  27.0 0.6 fusion.10
  27.6 0.6 convolution_add_fusion.7
  28.2 0.4 pad_maximum_fusion.2
  28.6 0.6 convolution_add_fusion.6
  29.2 0.6 convolution_add_fusion.5
  29.8 0.2 pad_maximum_fusion.4
  30.1 0.6 convolution_add_fusion.4
  30.7 0.4 pad_maximum_fusion.5
  31.1 0.6 convolution_add_fusion.3
  31.7 0.6 convolution_add_fusion.2
  32.3 0.5 pad_maximum_fusion.7
  32.8 0.6 convolution_add_fusion.1
  33.4 0.7 fusion.8
  34.0 0.1 reduce_sum.26
  34.1 0.1 reduce_sum.41
  34.3 0.1 reduce_sum.30
  34.4 0.1 reduce_sum.42
  34.5 16.1 %all-reduce.2 = (f32[1,32]{1,0:T(1,128)S(1)}, f32[1,32]{1,0:T(1,128)S(1)}) all-reduce(f32[1,32]{1,0:T(1,128)S(1)} %bitcast.103, f32[1,32]{1,0:T(1,128)S(1)} %bitcast.102), channel_id=1, replica_groups=mesh['dp'=4,'tm'=8] {'tm'}, use_global_device_ids=true, to_apply=%region_5.6 | all-reduce | flops 64 | bytes 512 | tf_op jit(solution)/shard_map/psum | solution.py:58
  50.6 0.1 mul.64
  50.7 0.1 mul.65
  50.9 0.1 sub.29
  51.0 0.4 multiply_convert_fusion
  51.4 0.1 pad.9
  51.5 1.4 slice.198
  52.9 1.4 slice.199
  54.3 1.5 slice.200
  55.8 1.4 slice.201
  57.2 1.4 slice.202
  58.6 1.5 %slice.203 = bf16[1,2,32,8,128]{4,3,2,1,0:T(8,128)(2,1)S(1)} slice(bf16[1,2,65,17,128]{4,3,2,1,0:T(8,128)(2,1)S(1)} %pad.9), slice={[0:1:1], [0:2:1], [1:64:2], [2:17:2], [0:128:1]} | slice | bytes 262144 | tf_op jit(solution)/shard_map/slice | solution.py:20
  60.2 2.3 %slice.204 = bf16[1,2,32,8,128]{4,3,2,1,0:T(8,128)(2,1)S(1)} slice(bf16[1,2,65,17,128]{4,3,2,1,0:T(8,128)(2,1)S(1)} %pad.9), slice={[0:1:1], [0:2:1], [2:65:2], [0:15:2], [0:128:1]} | slice | bytes 262144 | tf_op jit(solution)/shard_map/slice | solution.py:20
  62.5 2.3 %slice.205 = bf16[1,2,32,8,128]{4,3,2,1,0:T(8,128)(2,1)S(1)} slice(bf16[1,2,65,17,128]{4,3,2,1,0:T(8,128)(2,1)S(1)} %pad.9), slice={[0:1:1], [0:2:1], [2:65:2], [1:16:2], [0:128:1]} | slice | bytes 262144 | tf_op jit(solution)/shard_map/slice | solution.py:20
  64.8 2.9 %slice.206 = bf16[1,2,32,8,128]{4,3,2,1,0:T(8,128)(2,1)S(1)} slice(bf16[1,2,65,17,128]{4,3,2,1,0:T(8,128)(2,1)S(1)} %pad.9), slice={[0:1:1], [0:2:1], [2:65:2], [2:17:2], [0:128:1]} | slice | bytes 262144 | tf_op jit(solution)/shard_map/slice | solution.py:20
  68.0 0.6 copy.20
  68.6 1.3 fusion.11
  70.0 0.5 fusion.5
  70.5 0.7 copy.18
  71.1 3.4 %all-to-all-start = ((bf16[1,2,32,8,128]{4,3,1,0,2:T(8,128)(2,1)}), bf16[1,2,32,8,128]{4,3,1,0,2:T(8,128)(2,1)S(1)}, u32[]{:S(2)}, u32[]{:S(2)}) async-start(bf16[1,2,32,8,128]{4,3,1,0,2:T(8,128)(2,1)} %copy.18), calls=%async_computation | async-start | bytes 262144 | tf_op jit(solution)/shard_map/all_to_all | solution.py:76
  74.6 25.0 %reduce-scatter.2.cloned.1.call-done = f32[3,3,128,16]{2,3,1,0:T(8,128)} async-done(((f32[3,3,128,128]{2,3,1,0:T(8,128)}), f32[3,3,128,16]{2,3,1,0:T(8,128)}) %reduce-scatter.2.cloned.1.call-update) | async-done | bytes 73744 | tf_op jit(solution)/shard_map/reduce_scatter | solution.py:85
  99.6 0.7 copy.19
  100.2 41.1 %all-reduce.5.cloned.1.call-done = f32[3,3,128,16]{2,3,1,0:T(8,128)} async-done(((f32[3,3,128,16]{2,3,1,0:T(8,128)}), f32[3,3,128,16]{2,3,1,0:T(8,128)}) %all-reduce.5.cloned.1.call-update) | async-done | bytes 73744 | tf_op jit(solution)/shard_map/psum | solution.py:86
  141.3 1.5 %copy.37 = f32[3,3,128,16]{2,3,1,0:T(8,128)} copy(f32[3,3,128,16]{2,3,1,0:T(8,128)} %all-reduce.5.cloned.1.call-done) | data formatting | bytes 147456
  (28 shorter events, 0.6 us)
Async XLA Ops:
  7.2 62.8 %copy-start = (bf16[3,3,128,128]{3,2,1,0:T(8,128)(2,1)S(1)}, bf16[3,3,128,128]{3,2,1,0:T(8,128)(2,1)}, u32[]{:S(2)}) copy-start(bf16[3,3,128,128]{3,2,1,0:T(8,128)(2,1)} %param.10) | copy-start | bytes 884740
  7.2 15.5 %collective-permute-start = (bf16[1,2,64,16,128]{4,3,2,1,0:T(8,128)(2,1)}, bf16[1,2,64,16,128]{4,3,2,1,0:T(8,128)(2,1)S(1)}, u32[]{:S(2)}, u32[]{:S(2)}) collective-permute-start(bf16[1,2,64,16,128]{4,3,2,1,0:T(8,128)(2,1)} %param.6), channel_id=1, source_target_pairs={{0,1},{1,2},{2,3},{3,4},{4,5},{5,6},{6,7},{8,9},{9,10},{10,11},{11... | collective-permute-start | bytes 1572872 | tf_op jit(solution)/shard_map/ppermute | solution.py:12
  9.7 12.9 %all-to-all-start.1 = ((bf16[1,16,4,8,128]{4,3,2,0,1:T(8,128)(2,1)}), bf16[1,16,4,8,128]{4,3,2,0,1:T(8,128)(2,1)S(1)}, u32[]{:S(2)}, u32[]{:S(2)}) async-start(bf16[1,16,4,8,128]{4,3,2,0,1:T(8,128)(2,1)} %bitcast.100), calls=%async_computation.1 | async-start | bytes 262144 | tf_op jit(solution)/shard_map/all_to_all | solution.py:77
  15.8 6.9 %copy-start.1 = (bf16[1,2,64,16,128]{4,3,2,1,0:T(8,128)(2,1)S(1)}, bf16[1,2,64,16,128]{4,3,2,1,0:T(8,128)(2,1)}, u32[]{:S(2)}) copy-start(bf16[1,2,64,16,128]{4,3,2,1,0:T(8,128)(2,1)} %param.6) | copy-start | bytes 1572868
  15.9 83.7 %reduce-scatter.2.cloned.1.call-start = ((), (), s32[]{:S(2)}) async-start(), calls=%async_computation.3 | async-start | bytes 663552 | tf_op jit(solution)/shard_map/reduce_scatter | solution.py:85
  33.3 17.7 %copy-start.2 = (f32[128]{0:T(128)S(1)}, f32[128]{0:T(128)}, u32[]{:S(2)}) copy-start(f32[128]{0:T(128)} %param.9) | copy-start | bytes 1540
  33.4 17.7 %copy-start.3 = (f32[128]{0:T(128)S(1)}, f32[128]{0:T(128)}, u32[]{:S(2)}) copy-start(f32[128]{0:T(128)} %param.8) | copy-start | bytes 1540
  71.1 28.4 %all-to-all-start = ((bf16[1,2,32,8,128]{4,3,1,0,2:T(8,128)(2,1)}), bf16[1,2,32,8,128]{4,3,1,0,2:T(8,128)(2,1)S(1)}, u32[]{:S(2)}, u32[]{:S(2)}) async-start(bf16[1,2,32,8,128]{4,3,1,0,2:T(8,128)(2,1)} %copy.18), calls=%async_computation | async-start | bytes 262144 | tf_op jit(solution)/shard_map/all_to_all | solution.py:76
  74.5 66.8 %all-reduce.5.cloned.1.call-start = ((), (), s32[]{:S(2)}) async-start(), calls=%async_computation.4 | async-start | bytes 147456 | tf_op jit(solution)/shard_map/psum | solution.py:86
Sparse Core Ops, SparseCore 0:
  70.1 29.3 reduce-scatter.1
  102.4 38.8 all-reduce.4
where the time goes:
time: 150 us
  waiting for transfers between devices  71.4 us (48%)
  local copies, waits for them, and re-layouts  25.7 us (17%)
  blocking collectives  16.1 us (11%)
  between operations  14.5 us (10%)
  starting transfers between devices  12.1 us (8%)
  matrix products  7.17 us (5%)
  other arithmetic  2.62 us (2%)
    psum x1, waiting for transfers between devices, per_device(): grad_down = lax.psum(shares, 'dp')  41.1 us
    reduce_scatter x1, waiting for transfers between devices, per_device(): lax.psum_scatter(partial_value, 'tm', scatter_dimension=3, tiled=True)  25 us
    psum x1, blocking collectives, per_device(): group_sums, group_squares = lax.psum((group_sums, group_squares), 'tm')  16.1 us
    slice x9, local copies, waits for them, and re-layouts, down_patches(): extended[:, :, row_tap:row_tap + 2 * rows_out - 1:2, col_tap:col_tap + 2...  16 us
    all_to_all x1, starting transfers between devices, per_device(): lax.all_to_all(cotangent, 'tm', split_axis=1, concat_axis=2, tiled=True)  6.14 us
    dot_general x9, matrix products, per_device(): jnp.dot(stacked.reshape(-1, 3 * channels), tap_weight, preferred_element_...  5.38 us
    all_to_all x1, waiting for transfers between devices, per_device(): lax.all_to_all(cotangent, 'tm', split_axis=1, concat_axis=2, tiled=True)  5.37 us
    slice x2, local copies, waits for them, and re-layouts, per_device(): window_slab[:, time_tap:time_tap + frames_dev]  3.72 us
  transfers between devices with their start and end apart: 5, of which 3 were waited for; matrix products, arithmetic and copies ran while one was open for 2% of the time, Pallas kernels for 0%

commit v1 on v0

v1 whole, which is shorter than its diff:
```python
import functools

import jax
import jax.numpy as jnp
from jax import lax
from jax.experimental import pallas as pl
from jax.experimental.pallas import tpu as pltpu
from jax.sharding import PartitionSpec as P

G = 32
VMEM = pl.BlockSpec(memory_space=pltpu.VMEM)
ANY = pl.BlockSpec(memory_space=pl.ANY)
F32 = jnp.float32
BF16 = jnp.bfloat16


def passed_along(shard, axis, by):
    count = lax.axis_size(axis)
    pairs = [(i, i + by) for i in range(count) if 0 <= i + by < count]
    return lax.ppermute(shard, axis, pairs)


def exchanged(shard, axis, bits):
    count = lax.axis_size(axis)
    return lax.ppermute(shard, axis, [(i, i ^ bits) for i in range(count)])


def gather_taps(x_ref, lhs):
    _, height, width, chans = x_ref.shape
    zero = jnp.zeros((1, width, chans), x_ref.dtype)
    for f in range(2):
        frame = x_ref[f]
        views = (
            jnp.concatenate([zero, frame[: height - 1]], axis=0),
            frame,
            jnp.concatenate([frame[1:], zero], axis=0),
        )
        for p in range(3):
            col = (3 * f + p) * chans
            lhs[:, col : col + chans] = views[p].reshape(height * width, chans)


def shifted_sum(wide, width):
    rows, lanes = wide.shape
    lanes = lanes // 3
    col = lax.broadcasted_iota(jnp.int32, (rows, lanes), 0) % width
    left = jnp.where(col == 0, 0.0, pltpu.roll(wide[:, :lanes], 1, 0))
    right = jnp.where(col == width - 1, 0.0, pltpu.roll(wide[:, 2 * lanes :], rows - 1, 0))
    return left + wide[:, lanes : 2 * lanes] + right


def own_kernel(x_ref, w_hbm, part_ref, early_ref, lhs, late, sems):
    _, height, width, chans = x_ref.shape
    copies = []
    for f in range(4):
        target = late if f >= 2 else early_ref
        for t in range(2):
            tap = f - t
            for q in range(3):
                cols = pl.ds((2 * q + t) * chans, chans)
                if 0 <= tap <= 2:
                    copy = pltpu.make_async_copy(
                        w_hbm.at[tap, :, q], target.at[f % 2, :, :, cols], sems.at[len(copies)]
                    )
                    copy.start()
                    copies.append(copy)
                else:
                    target[f % 2, :, :, cols] = jnp.zeros((3, chans, chans), BF16)
    gather_taps(x_ref, lhs)
    for copy in copies:
        copy.wait()
    weights = late[...].reshape(6 * chans, 6 * chans)
    block = 256
    for r in range(0, height * width, block):
        wide = jnp.dot(lhs[r : r + block], weights, preferred_element_type=F32)
        both = shifted_sum(wide, width)
        for t in range(2):
            part_ref[t, r : r + block] = both[:, t * chans : (t + 1) * chans]


def conv_kernel(x_ref, w_ref, part_ref, conv_ref, stats_ref, lhs):
    _, height, width, chans = x_ref.shape
    gather_taps(x_ref, lhs)
    weights = w_ref[...].reshape(6 * chans, 6 * chans)
    block = 256
    total = jnp.zeros((1, chans), F32)
    squares = jnp.zeros((1, chans), F32)
    for r in range(0, height * width, block):
        wide = jnp.dot(lhs[r : r + block], weights, preferred_element_type=F32)
        both = shifted_sum(wide, width)
        for t in range(2):
            value = both[:, t * chans : (t + 1) * chans] + part_ref[t, r : r + block]
            conv_ref[t, r : r + block] = value
            total = total + jnp.sum(value, axis=0, keepdims=True)
            squares = squares + jnp.sum(value * value, axis=0, keepdims=True)
    tile = jnp.concatenate([total, squares, jnp.zeros((6, chans), F32)], axis=0)
    for k in range(stats_ref.shape[0]):
        stats_ref[k] = tile


def group_sum(tile, size):
    lanes = tile.shape[-1]
    lane = lax.broadcasted_iota(jnp.int32, tile.shape, 1)
    step = 1
    while step < size:
        up = pltpu.roll(tile, lanes - step, 1)
        down = pltpu.roll(tile, step, 1)
        tile = tile + jnp.where((lane // step) % 2 == 0, up, down)
        step *= 2
    return tile


def down_kernel(members, width, conv_ref, stats_ref, affine_ref, w_ref, cot_ref, enc_ref, grad_ref, patch):
    frames, cells, chans = conv_ref.shape
    rows = cells // width
    half = width // 2
    sums = stats_ref[0]
    for k in range(1, stats_ref.shape[0]):
        sums = sums + stats_ref[k]
    sums = group_sum(sums, chans // G) / members
    mean = sums[0:1]
    variance = sums[1:2] - mean * mean
    scale = lax.rsqrt(variance + 1e-06) * affine_ref[0:1] * 0.5
    shift = affine_ref[1:2] * 0.5

    def silu(value):
        u = (value - mean) * scale + shift
        return u + u * jnp.tanh(u)

    outs = rows // 2 * half
    for t in range(frames):
        even = silu(conv_ref[t, pl.ds(0, rows * half, stride=2)])
        odd = silu(conv_ref[t, pl.ds(1, rows * half, stride=2)])
        col = lax.broadcasted_iota(jnp.int32, even.shape, 0) % half
        after = jnp.where(col == half - 1, 0.0, pltpu.roll(even, rows * half - 1, 0))
        for q, cells_q in enumerate((even, odd, after)):
            split = cells_q.reshape(rows // 2, 2, half, chans)
            below = jnp.concatenate([split[1:, 0], jnp.zeros((1, half, chans), F32)], axis=0)
            for p, view in enumerate((split[:, 0], split[:, 1], below)):
                tap = (3 * p + q) * chans
                patch[t * outs : (t + 1) * outs, tap : tap + chans] = view.reshape(outs, chans).astype(BF16)
    values = patch[...]
    enc_ref[...] = jnp.dot(values, w_ref[...], preferred_element_type=F32).astype(BF16)
    grad = lax.dot_general(cot_ref[...], values, (((0,), (0,)), ((), ())), preferred_element_type=F32)
    for tap in range(9):
        grad_ref[tap] = grad[:, tap * chans : (tap + 1) * chans].astype(BF16)


def pick(array, index, axis):
    return lax.dynamic_index_in_dim(array, index, axis, keepdims=False)


def joined(mine, other, bit, axis):
    low = jnp.where(bit == 0, mine, other)
    high = jnp.where(bit == 0, other, mine)
    return jnp.stack([low, high], axis=axis)


def per_device(activations, conv_weight, norm_gain, norm_bias, down_weight, cotangent):
    _, frames, height, width, chans = activations.shape
    n = lax.axis_size("tm")
    bits = n.bit_length() - 1
    me = lax.axis_index("tm")
    bit = [(me >> s) & 1 for s in range(bits)]
    cells = height * width
    half_cells = (height // 2) * (width // 2)
    params = pltpu.CompilerParams(vmem_limit_bytes=32 * 1024 * 1024)
    own = activations[0]

    earlier = passed_along(own, "tm", 1)

    rows_dev = (height // 2) // n
    cot = cotangent.reshape((2,) * bits + (frames, rows_dev * (width // 2), chans))
    for s in range(bits):
        axis = bits - 1 - s
        other = exchanged(pick(cot, 1 - bit[s], axis), "tm", 1 << s)
        cot = joined(pick(cot, bit[s], axis), other, bit[s], axis + 1)
    cot = cot.reshape(frames * half_cells, chans)

    part, early = pl.pallas_call(
        own_kernel,
        out_shape=(
            jax.ShapeDtypeStruct((frames, cells, chans), F32),
            jax.ShapeDtypeStruct((2, 3, chans, 6 * chans), BF16),
        ),
        in_specs=[VMEM, ANY],
        out_specs=(VMEM, VMEM),
        scratch_shapes=[
            pltpu.VMEM((cells, 6 * chans), BF16),
            pltpu.VMEM((2, 3, chans, 6 * chans), BF16),
            pltpu.SemaphoreType.DMA((18,)),
        ],
        compiler_params=params,
        cost_estimate=pl.CostEstimate(flops=2 * cells * 36 * chans * chans, bytes_accessed=2**21, transcendentals=0),
        name="own_frames",
    )(own, conv_weight)

    conv, stats = pl.pallas_call(
        conv_kernel,
        out_shape=(
            jax.ShapeDtypeStruct((frames, cells, chans), F32),
            jax.ShapeDtypeStruct((n, 8, chans), F32),
        ),
        in_specs=[VMEM, VMEM, VMEM],
        out_specs=(VMEM, VMEM),
        scratch_shapes=[pltpu.VMEM((cells, 6 * chans), BF16)],
        compiler_params=params,
        cost_estimate=pl.CostEstimate(flops=2 * cells * 36 * chans * chans, bytes_accessed=2**21, transcendentals=0),
        name="earlier_frames",
    )(earlier, early, part)

    stats = lax.all_to_all(stats, "tm", split_axis=0, concat_axis=0, tiled=True)
    affine = jnp.stack([norm_gain, norm_bias])
    members = float(frames * n * cells * (chans // G))

    enc, grad = pl.pallas_call(
        functools.partial(down_kernel, members, width),
        out_shape=(
            jax.ShapeDtypeStruct((frames * half_cells, chans), BF16),
            jax.ShapeDtypeStruct((9, chans, chans), BF16),
        ),
        in_specs=[VMEM] * 5,
        out_specs=(VMEM, VMEM),
        scratch_shapes=[pltpu.VMEM((frames * half_cells, 9 * chans), BF16)],
        compiler_params=params,
        name="down",
    )(conv, stats, affine, down_weight.reshape(9 * chans, chans), cot)

    share = chans // n
    grad = grad.reshape((9,) + (2,) * bits + (share, chans))
    enc = enc.reshape((frames,) + (2,) * bits + (rows_dev * (width // 2), chans))
    for s in range(bits):
        axis = bits - s
        keep_g, send_g = pick(grad, bit[s], axis), pick(grad, 1 - bit[s], axis)
        keep_e, send_e = pick(enc, bit[s], axis), pick(enc, 1 - bit[s], axis)
        packed = jnp.concatenate([send_g.reshape(-1, chans), send_e.reshape(-1, chans)], axis=0)
        packed = exchanged(packed, "tm", 1 << s)
        cut = send_g.size // chans
        grad = (keep_g.astype(F32) + packed[:cut].reshape(keep_g.shape).astype(F32)).astype(BF16)
        enc = joined(keep_e, packed[cut:].reshape(keep_e.shape), bit[s], 0)
        enc = enc.reshape((-1,) + keep_e.shape[1:])
    encoded = enc.reshape(1, frames * n, rows_dev, width // 2, chans)

    dp = lax.axis_size("dp")
    terms = [grad.astype(F32)] + [exchanged(grad, "dp", b).astype(F32) for b in range(1, dp)]
    while len(terms) > 1:
        terms = [terms[i] + terms[i + 1] for i in range(0, len(terms), 2)]
    grad_down = jnp.swapaxes(terms[0], 1, 2).reshape(3, 3, chans, share)
    return encoded, grad_down


def solution(mesh):
    placed = (P("dp", "tm", None, None, None), P(), P(), P(), P(), P("dp", None, "tm", None, None))
    return jax.shard_map(
        per_device,
        mesh=mesh,
        in_specs=placed,
        out_specs=(P("dp", None, "tm", None, None), P(None, None, None, "tm")),
        check_vma=False,
    )
```

time: 150 us -> 55.4 us (0.37)
  waiting for transfers between devices: 71.4 us -> 25.4 us
  local copies, waits for them, and re-layouts: 25.7 us -> 3.21 us
  blocking collectives: 16.1 us -> 0 us
  between operations: 14.5 us -> 0.91 us
  matrix products: 7.17 us -> 0 us
  starting transfers between devices: 12.1 us -> 17.8 us
  Pallas kernels: 0 us -> 5.29 us
    psum x1 -> x0, waiting for transfers between devices: 41.1 us -> none  [per_device(): grad_down = lax.psum(shares, 'dp')]
    reduce_scatter x1 -> x0, waiting for transfers between devices: 25 us -> none  [per_device(): lax.psum_scatter(partial_value, 'tm', scatter_dimension=3, tiled=True)]
    slice x12 -> x6, local copies, waits for them, and re-layouts: 21.1 us -> 0.04 us  [the longest x3 0.02 us: per_device(): packed[:cut].reshape(keep_g.shape).astype(F32)]
    ppermute x0 -> x9, waiting for transfers between devices: none -> 19.6 us  [exchanged(): return lax.ppermute(shard, axis, [(i, i ^ bits) for i in range(count)])]
    psum x1 -> x0, blocking collectives: 16.1 us -> none  [per_device(): group_sums, group_squares = lax.psum((group_sums, group_squares), 'tm')]
    ppermute x0 -> x9, starting transfers between devices: none -> 11.1 us  [exchanged(): return lax.ppermute(shard, axis, [(i, i ^ bits) for i in range(count)])]
    dot_general x11 -> x0, matrix products: 7.17 us -> none  [the longest x9 5.38 us: per_device(): jnp.dot(stacked.reshape(-1, 3 * channels), tap_weight, preferred_element_...]
    pallas_call x0 -> x3, Pallas kernels: none -> 5.29 us  [the longest x1 2.17 us: per_device(): pl.pallas_call(own_kernel, out_shape=(jax.ShapeDtypeStruct((frames, cells...]
  transfers between devices with their start and end apart: 5 -> 11, of which waited for: 3 -> 8; matrix products, arithmetic and copies ran while one was open for 2% -> 3% of each run, Pallas kernels for 0% -> 4%
where the time goes in v1:
time: 55.4 us; the launch traced here: 55 us
  waiting for transfers between devices  25.4 us (46%)
  starting transfers between devices  17.8 us (32%)
  Pallas kernels  5.29 us (10%)
  local copies, waits for them, and re-layouts  3.21 us (6%)
  other arithmetic  2.48 us (4%)
  between operations  0.91 us (2%)
    ppermute x9, waiting for transfers between devices, exchanged(): return lax.ppermute(shard, axis, [(i, i ^ bits) for i in range(count)])  19.6 us
    ppermute x9, starting transfers between devices, exchanged(): return lax.ppermute(shard, axis, [(i, i ^ bits) for i in range(count)])  11.1 us
    all_to_all x1, waiting for transfers between devices, per_device(): stats = lax.all_to_all(stats, 'tm', split_axis=0, concat_axis=0, tiled=True)  5.72 us
    all_to_all x1, starting transfers between devices, per_device(): stats = lax.all_to_all(stats, 'tm', split_axis=0, concat_axis=0, tiled=True)  4.71 us
    unnamed x10, local copies, waits for them, and re-layouts  2.22 us
    pallas_call x1, Pallas kernels, per_device(): pl.pallas_call(own_kernel, out_shape=(jax.ShapeDtypeStruct((frames, cells...  2.17 us
    pallas_call x1, Pallas kernels, per_device(): pl.pallas_call(conv_kernel, out_shape=(jax.ShapeDtypeStruct((frames, cell...  2.13 us
    ppermute x1, starting transfers between devices, passed_along(): return lax.ppermute(shard, axis, pairs)  1.98 us
  transfers between devices with their start and end apart: 11, of which 8 were waited for; matrix products, arithmetic and copies ran while one was open for 3% of the time, Pallas kernels for 4%

profile of v1, /device:TPU:0, one launch (start us, length us, event | category | flops | bytes accessed | tf_op | source)
XLA Modules:
  0.0 55.0 jit_solution(5555905522506682925)
XLA Ops:
  0.6 0.9 %dynamic-slice_bitcast_fusion = bf16[2,2,2,32,128]{4,3,2,1,0:T(8,128)(2,1)S(1)} fusion(bf16[2,2,2,2,32,128]{5,4,3,2,1,0:T(8,128)(2,1)} %bitcast.115, s32[]{:T(128)S(6)} %select_n.154), kind=kLoop, calls=%fused_computation.45 | loop fusion | bytes 131076 | tf_op jit(solution)/shard_map/jit(dynamic_index_in_dim)/squeeze | solution.py:150
  1.5 0.5 collective-permute-start.1
  1.9 2.0 %collective-permute-start = (bf16[2,64,16,128]{3,2,1,0:T(8,128)(2,1)}, bf16[2,64,16,128]{3,2,1,0:T(8,128)(2,1)S(1)}, u32[]{:S(2)}, u32[]{:S(2)}) collective-permute-start(bf16[2,64,16,128]{3,2,1,0:T(8,128)(2,1)} %bitcast.96), channel_id=1, source_target_pairs={{0,1},{1,2},{2,3},{3,4},{4,5},{5,6},{6,7},{8,9},{9,10},{10,11},{11... | collective-permute-start | bytes 1572872 | tf_op jit(solution)/shard_map/ppermute | solution.py:20
  4.0 0.0 collective-permute-done.1
  4.0 0.9 %fusion.12 = (bf16[2,2,2,1,32,128]{5,4,2,1,0,3:T(8,128)(2,1)S(1)}, bf16[2,2,2,1,32,128]{5,4,2,1,0,3:T(8,128)(2,1)S(1)}) fusion(bf16[2,2,2,32,128]{4,3,2,1,0:T(8,128)(2,1)S(1)} %collective-permute-done.1, pred[]{:T(512)S(6)} %eq.8, bf16[2,2,2,2,32,128]{5,4,3,2,1,0:T(8,128)(2,1)} %bitcast.116, s32[]{:T(128)S(6)} %select_n.153), kind=kLoop, calls=%fused_computation.41 | loop fusion | flops 65536 | bytes 262149 | tf_op jit(solution)/shard_map/stack | solution.py:156
  4.9 3.1 %collective-permute-start.2 = (bf16[2,2,2,32,128]{4,3,2,1,0:T(8,128)(2,1)S(1)}, bf16[2,2,2,32,128]{4,3,2,1,0:T(8,128)(2,1)S(1)}, u32[]{:S(2)}, u32[]{:S(2)}) collective-permute-start(bf16[2,2,2,32,128]{4,3,2,1,0:T(8,128)(2,1)S(1)} %bitcast.118), channel_id=1, source_target_pairs={{0,2},{1,3},{2,0},{3,1},{4,6},{5,7},{6,4},{7,5},{8,10},{9,11},{10,... | collective-permute-start | bytes 196616 | tf_op jit(solution)/shard_map/ppermute | solution.py:25
  7.9 0.0 copy-start.1
  7.9 1.2 %copy-done.1 = bf16[3,3,3,128,128]{4,3,2,1,0:T(8,128)(2,1)S(1)} copy-done((bf16[3,3,3,128,128]{4,3,2,1,0:T(8,128)(2,1)S(1)}, bf16[3,3,3,128,128]{4,3,2,1,0:T(8,128)(2,1)}, u32[]{:S(2)}) %copy-start.1) | copy-done | bytes 884760
  9.1 0.0 copy-start.2
  9.1 1.0 %copy-done.2 = bf16[1,2,64,16,128]{4,3,2,1,0:T(8,128)(2,1)S(1)} copy-done((bf16[1,2,64,16,128]{4,3,2,1,0:T(8,128)(2,1)S(1)}, bf16[1,2,64,16,128]{4,3,2,1,0:T(8,128)(2,1)}, u32[]{:S(2)}) %copy-start.2) | copy-done | bytes 524312
  10.1 0.0 copy-start.3
  10.1 0.0 copy-start.4
  10.1 2.2 %own_frames.1 = (f32[2,1024,128]{2,1,0:T(8,128)S(1)}, bf16[2,3,128,768]{3,2,1,0:T(8,128)(2,1)S(1)}) custom-call(bf16[2,64,16,128]{3,2,1,0:T(8,128)(2,1)S(1)} %bitcast.97, bf16[3,3,3,128,128]{4,3,2,1,0:T(8,128)(2,1)S(1)} %copy-done.1), custom_call_target="tpu_custom_call" | custom-call | flops 1207959552 | bytes 2097152 | tf_op jit(solution)/shard_map/own_frames/pallas_call | solution.py:180
  12.3 0.0 collective-permute-done.2
  12.4 2.7 %collective-permute-start.3 = (bf16[2,2,2,32,128]{4,3,2,1,0:T(8,128)(2,1)S(1)}, bf16[2,2,2,32,128]{4,3,2,1,0:T(8,128)(2,1)S(1)}, u32[]{:S(2)}, u32[]{:S(2)}) collective-permute-start(bf16[2,2,2,32,128]{4,3,2,1,0:T(8,128)(2,1)S(1)} %fusion.4), channel_id=1, source_target_pairs={{0,4},{1,5},{2,6},{3,7},{4,0},{5,1},{6,2},{7,3},{8,12},{9,13},{10,... | collective-permute-start | bytes 196616 | tf_op jit(solution)/shard_map/ppermute | solution.py:25
  15.0 0.0 copy-done.3
  15.0 0.0 copy-done.4
  15.1 3.7 %collective-permute-done.3 = bf16[2,2,2,32,128]{4,3,2,1,0:T(8,128)(2,1)S(1)} collective-permute-done((bf16[2,2,2,32,128]{4,3,2,1,0:T(8,128)(2,1)S(1)}, bf16[2,2,2,32,128]{4,3,2,1,0:T(8,128)(2,1)S(1)}, u32[]{:S(2)}, u32[]{:S(2)}) %collective-permute-start.3) | collective-permute-done | bytes 65568 | tf_op jit(solution)/shard_map/ppermute | solution.py:25
  18.8 0.0 collective-permute-done.x_ref
  18.8 0.0 copy-start
  18.8 2.1 %earlier_frames.1 = (f32[2,1024,128]{2,1,0:T(8,128)S(1)}, f32[8,8,128]{2,1,0:T(8,128)}) custom-call(bf16[2,64,16,128]{3,2,1,0:T(8,128)(2,1)S(1)} %collective-permute-done.x_ref, bf16[2,3,128,768]{3,2,1,0:T(8,128)(2,1)S(1)} %get-tuple-element.8.w_ref, f32[2,1024,128]{2,1,0:T(8,128)S(1)} %get-tuple-element.9.part_ref), custom_call_target="tpu_custom_call" | custom-call | flops 1207959552 | bytes 2097152 | tf_op jit(solution)/shard_map/earlier_frames/pallas_call | solution.py:198
  20.9 4.7 %all-to-all-start = ((f32[8,8,128]{2,1,0:T(8,128)}), f32[8,8,128]{2,1,0:T(8,128)S(1)}, u32[]{:S(2)}, u32[]{:S(2)}) async-start(f32[8,8,128]{2,1,0:T(8,128)} %get-tuple-element.11), calls=%async_computation | async-start | bytes 65536 | tf_op jit(solution)/shard_map/all_to_all | solution.py:212
  25.7 5.7 %all-to-all-done.stats_ref = f32[8,8,128]{2,1,0:T(8,128)S(1)} async-done(((f32[8,8,128]{2,1,0:T(8,128)}), f32[8,8,128]{2,1,0:T(8,128)S(1)}, u32[]{:S(2)}, u32[]{:S(2)}) %all-to-all-start) | async-done | bytes 32800 | tf_op jit(solution)/shard_map/all_to_all | solution.py:212
  31.4 0.0 copy-done
  31.4 1.0 %down.1 = (bf16[512,128]{1,0:T(8,128)(2,1)S(1)}, bf16[9,128,128]{2,1,0:T(8,128)(2,1)S(1)}) custom-call(f32[2,1024,128]{2,1,0:T(8,128)S(1)} %get-tuple-element.10.conv_ref, f32[8,8,128]{2,1,0:T(8,128)S(1)} %all-to-all-done.stats_ref, f32[2,128]{1,0:T(2,128)S(1)} %pad_maximum_fusion.7.affine_ref, bf16[1152,128]{1,0:T(8,128)(2,1)S(1)} %bitcast.91, ...), custom_call_target="tpu_custom_call" | custom-call | tf_op jit(solution)/shard_map/down/pallas_call | solution.py:216
  32.5 0.1 collective-permute-start.4
  32.5 1.5 %collective-permute-done.4 = bf16[832,128]{1,0:T(8,128)(2,1)S(1)} collective-permute-done((bf16[832,128]{1,0:T(8,128)(2,1)S(1)}, bf16[832,128]{1,0:T(8,128)(2,1)S(1)}, u32[]{:S(2)}, u32[]{:S(2)}) %collective-permute-start.4) | collective-permute-done | bytes 213024 | tf_op jit(solution)/shard_map/ppermute | solution.py:25
  34.2 0.7 %collective-permute-start.5 = (bf16[544,128]{1,0:T(8,128)(2,1)S(1)}, bf16[544,128]{1,0:T(8,128)(2,1)S(1)}, u32[]{:S(2)}, u32[]{:S(2)}) collective-permute-start(bf16[544,128]{1,0:T(8,128)(2,1)S(1)} %pad_maximum_fusion.1), channel_id=1, source_target_pairs={{0,2},{1,3},{2,0},{3,1},{4,6},{5,7},{6,4},{7,5},{8,10},{9,11},{10,... | collective-permute-start | bytes 417800 | tf_op jit(solution)/shard_map/ppermute | solution.py:25
  34.9 5.1 %collective-permute-done.5 = bf16[544,128]{1,0:T(8,128)(2,1)S(1)} collective-permute-done((bf16[544,128]{1,0:T(8,128)(2,1)S(1)}, bf16[544,128]{1,0:T(8,128)(2,1)S(1)}, u32[]{:S(2)}, u32[]{:S(2)}) %collective-permute-start.5) | collective-permute-done | bytes 139296 | tf_op jit(solution)/shard_map/ppermute | solution.py:25
  40.1 0.6 %collective-permute-start.6 = (bf16[400,128]{1,0:T(8,128)(2,1)S(1)}, bf16[400,128]{1,0:T(8,128)(2,1)S(1)}, u32[]{:S(2)}, u32[]{:S(2)}) collective-permute-start(bf16[400,128]{1,0:T(8,128)(2,1)S(1)} %pad_maximum_fusion.6), channel_id=1, source_target_pairs={{0,4},{1,5},{2,6},{3,7},{4,0},{5,1},{6,2},{7,3},{8,12},{9,13},{10,... | collective-permute-start | bytes 307208 | tf_op jit(solution)/shard_map/ppermute | solution.py:25
  40.7 6.7 %collective-permute-done.6 = bf16[400,128]{1,0:T(8,128)(2,1)S(1)} collective-permute-done((bf16[400,128]{1,0:T(8,128)(2,1)S(1)}, bf16[400,128]{1,0:T(8,128)(2,1)S(1)}, u32[]{:S(2)}, u32[]{:S(2)}) %collective-permute-start.6) | collective-permute-done | bytes 102432 | tf_op jit(solution)/shard_map/ppermute | solution.py:25
  47.4 2.5 %collective-permute-start.9 = (bf16[9,16,128]{2,1,0:T(8,128)(2,1)S(1)}, bf16[9,16,128]{2,1,0:T(8,128)(2,1)S(1)}, u32[]{:S(2)}, u32[]{:S(2)}) collective-permute-start(bf16[9,16,128]{2,1,0:T(8,128)(2,1)S(1)} %fusion.2), channel_id=1, source_target_pairs={{0,24},{8,16},{16,8},{24,0},{1,25},{9,17},{17,9},{25,1},{2,26},{10... | collective-permute-start | bytes 110600 | tf_op jit(solution)/shard_map/ppermute | solution.py:25
  49.9 0.5 collective-permute-start.8
  50.4 0.5 collective-permute-start.7
  51.0 0.7 %pad_maximum_fusion.5 = bf16[2,8,32,128]{3,2,1,0:T(8,128)(2,1)} fusion(bf16[1,8,32,128]{3,2,1,0:T(8,128)(2,1)S(1)} %get-tuple-element.15, bf16[1,8,32,128]{3,2,1,0:T(8,128)(2,1)S(1)} %get-tuple-element.14), kind=kLoop, calls=%fused_computation.17 | loop fusion | flops 65536 | bytes 262144 | tf_op jit(solution)/shard_map/stack | solution.py:156
  51.6 0.8 %collective-permute-done.9 = bf16[9,16,128]{2,1,0:T(8,128)(2,1)S(1)} collective-permute-done((bf16[9,16,128]{2,1,0:T(8,128)(2,1)S(1)}, bf16[9,16,128]{2,1,0:T(8,128)(2,1)S(1)}, u32[]{:S(2)}, u32[]{:S(2)}) %collective-permute-start.9) | collective-permute-done | bytes 36896 | tf_op jit(solution)/shard_map/ppermute | solution.py:25
  52.4 1.4 %collective-permute-done.8 = bf16[9,16,128]{2,1,0:T(8,128)(2,1)S(1)} collective-permute-done((bf16[9,16,128]{2,1,0:T(8,128)(2,1)S(1)}, bf16[9,16,128]{2,1,0:T(8,128)(2,1)S(1)}, u32[]{:S(2)}, u32[]{:S(2)}) %collective-permute-start.8) | collective-permute-done | bytes 36896 | tf_op jit(solution)/shard_map/ppermute | solution.py:25
  53.9 0.5 collective-permute-done.7
  54.4 0.7 %add_add_fusion = f32[9,16,128]{2,1,0:T(8,128)} fusion(bf16[9,16,128]{2,1,0:T(8,128)(2,1)S(1)} %collective-permute-done.9, bf16[9,16,128]{2,1,0:T(8,128)(2,1)S(1)} %collective-permute-done.8, bf16[9,16,128]{2,1,0:T(8,128)(2,1)S(1)} %collective-permute-done.7, bf16[9,16,128]{2,1,0:T(8,128)(2,1)S(1)} %fusion.2), kind=kLoop, calls=%fused_computation.21 | loop fusion | flops 129024 | bytes 221184 | tf_op jit(solution)/shard_map/add | solution.py:247
  (30 shorter events, 0.4 us)
Async XLA Ops:
  1.5 2.5 %collective-permute-start.1 = (bf16[2,2,2,32,128]{4,3,2,1,0:T(8,128)(2,1)S(1)}, bf16[2,2,2,32,128]{4,3,2,1,0:T(8,128)(2,1)S(1)}, u32[]{:S(2)}, u32[]{:S(2)}) collective-permute-start(bf16[2,2,2,32,128]{4,3,2,1,0:T(8,128)(2,1)S(1)} %dynamic-slice_bitcast_fusion), channel_id=1, source_target_pairs={{0,1},{1,0},{2,3},{3,2},{4,5},{5,4},{6,7},{7,6},{8,9},{9,8},{10,11... | collective-permute-start | bytes 196616 | tf_op jit(solution)/shard_map/ppermute | solution.py:25
  1.9 16.8 %collective-permute-start = (bf16[2,64,16,128]{3,2,1,0:T(8,128)(2,1)}, bf16[2,64,16,128]{3,2,1,0:T(8,128)(2,1)S(1)}, u32[]{:S(2)}, u32[]{:S(2)}) collective-permute-start(bf16[2,64,16,128]{3,2,1,0:T(8,128)(2,1)} %bitcast.96), channel_id=1, source_target_pairs={{0,1},{1,2},{2,3},{3,4},{4,5},{5,6},{6,7},{8,9},{9,10},{10,11},{11... | collective-permute-start | bytes 1572872 | tf_op jit(solution)/shard_map/ppermute | solution.py:20
  4.9 7.5 %collective-permute-start.2 = (bf16[2,2,2,32,128]{4,3,2,1,0:T(8,128)(2,1)S(1)}, bf16[2,2,2,32,128]{4,3,2,1,0:T(8,128)(2,1)S(1)}, u32[]{:S(2)}, u32[]{:S(2)}) collective-permute-start(bf16[2,2,2,32,128]{4,3,2,1,0:T(8,128)(2,1)S(1)} %bitcast.118), channel_id=1, source_target_pairs={{0,2},{1,3},{2,0},{3,1},{4,6},{5,7},{6,4},{7,5},{8,10},{9,11},{10,... | collective-permute-start | bytes 196616 | tf_op jit(solution)/shard_map/ppermute | solution.py:25
  7.9 1.2 %copy-start.1 = (bf16[3,3,3,128,128]{4,3,2,1,0:T(8,128)(2,1)S(1)}, bf16[3,3,3,128,128]{4,3,2,1,0:T(8,128)(2,1)}, u32[]{:S(2)}) copy-start(bf16[3,3,3,128,128]{4,3,2,1,0:T(8,128)(2,1)} %w_hbm.1) | copy-start | bytes 2654212
  9.1 1.0 %copy-start.2 = (bf16[1,2,64,16,128]{4,3,2,1,0:T(8,128)(2,1)S(1)}, bf16[1,2,64,16,128]{4,3,2,1,0:T(8,128)(2,1)}, u32[]{:S(2)}) copy-start(bf16[1,2,64,16,128]{4,3,2,1,0:T(8,128)(2,1)} %param.6) | copy-start | bytes 1572868
  10.1 4.9 %copy-start.3 = (f32[128]{0:T(128)S(1)}, f32[128]{0:T(128)}, u32[]{:S(2)}) copy-start(f32[128]{0:T(128)} %param.9) | copy-start | bytes 1540
  10.1 4.9 %copy-start.4 = (f32[128]{0:T(128)S(1)}, f32[128]{0:T(128)}, u32[]{:S(2)}) copy-start(f32[128]{0:T(128)} %param.8) | copy-start | bytes 1540
  12.4 6.4 %collective-permute-start.3 = (bf16[2,2,2,32,128]{4,3,2,1,0:T(8,128)(2,1)S(1)}, bf16[2,2,2,32,128]{4,3,2,1,0:T(8,128)(2,1)S(1)}, u32[]{:S(2)}, u32[]{:S(2)}) collective-permute-start(bf16[2,2,2,32,128]{4,3,2,1,0:T(8,128)(2,1)S(1)} %fusion.4), channel_id=1, source_target_pairs={{0,4},{1,5},{2,6},{3,7},{4,0},{5,1},{6,2},{7,3},{8,12},{9,13},{10,... | collective-permute-start | bytes 196616 | tf_op jit(solution)/shard_map/ppermute | solution.py:25
  18.8 12.6 %copy-start = (bf16[3,3,128,128]{3,2,1,0:T(8,128)(2,1)S(1)}, bf16[3,3,128,128]{3,2,1,0:T(8,128)(2,1)}, u32[]{:S(2)}) copy-start(bf16[3,3,128,128]{3,2,1,0:T(8,128)(2,1)} %param.10) | copy-start | bytes 884740
  20.9 10.5 %all-to-all-start = ((f32[8,8,128]{2,1,0:T(8,128)}), f32[8,8,128]{2,1,0:T(8,128)S(1)}, u32[]{:S(2)}, u32[]{:S(2)}) async-start(f32[8,8,128]{2,1,0:T(8,128)} %get-tuple-element.11), calls=%async_computation | async-start | bytes 65536 | tf_op jit(solution)/shard_map/all_to_all | solution.py:212
  32.5 1.5 %collective-permute-start.4 = (bf16[832,128]{1,0:T(8,128)(2,1)S(1)}, bf16[832,128]{1,0:T(8,128)(2,1)S(1)}, u32[]{:S(2)}, u32[]{:S(2)}) collective-permute-start(bf16[832,128]{1,0:T(8,128)(2,1)S(1)} %pad_maximum_fusion), channel_id=1, source_target_pairs={{0,1},{1,0},{2,3},{3,2},{4,5},{5,4},{6,7},{7,6},{8,9},{9,8},{10,11... | collective-permute-start | bytes 638984 | tf_op jit(solution)/shard_map/ppermute | solution.py:25
  34.2 5.8 %collective-permute-start.5 = (bf16[544,128]{1,0:T(8,128)(2,1)S(1)}, bf16[544,128]{1,0:T(8,128)(2,1)S(1)}, u32[]{:S(2)}, u32[]{:S(2)}) collective-permute-start(bf16[544,128]{1,0:T(8,128)(2,1)S(1)} %pad_maximum_fusion.1), channel_id=1, source_target_pairs={{0,2},{1,3},{2,0},{3,1},{4,6},{5,7},{6,4},{7,5},{8,10},{9,11},{10,... | collective-permute-start | bytes 417800 | tf_op jit(solution)/shard_map/ppermute | solution.py:25
  40.1 7.3 %collective-permute-start.6 = (bf16[400,128]{1,0:T(8,128)(2,1)S(1)}, bf16[400,128]{1,0:T(8,128)(2,1)S(1)}, u32[]{:S(2)}, u32[]{:S(2)}) collective-permute-start(bf16[400,128]{1,0:T(8,128)(2,1)S(1)} %pad_maximum_fusion.6), channel_id=1, source_target_pairs={{0,4},{1,5},{2,6},{3,7},{4,0},{5,1},{6,2},{7,3},{8,12},{9,13},{10,... | collective-permute-start | bytes 307208 | tf_op jit(solution)/shard_map/ppermute | solution.py:25
  47.4 5.0 %collective-permute-start.9 = (bf16[9,16,128]{2,1,0:T(8,128)(2,1)S(1)}, bf16[9,16,128]{2,1,0:T(8,128)(2,1)S(1)}, u32[]{:S(2)}, u32[]{:S(2)}) collective-permute-start(bf16[9,16,128]{2,1,0:T(8,128)(2,1)S(1)} %fusion.2), channel_id=1, source_target_pairs={{0,24},{8,16},{16,8},{24,0},{1,25},{9,17},{17,9},{25,1},{2,26},{10... | collective-permute-start | bytes 110600 | tf_op jit(solution)/shard_map/ppermute | solution.py:25
  49.9 4.0 %collective-permute-start.8 = (bf16[9,16,128]{2,1,0:T(8,128)(2,1)S(1)}, bf16[9,16,128]{2,1,0:T(8,128)(2,1)S(1)}, u32[]{:S(2)}, u32[]{:S(2)}) collective-permute-start(bf16[9,16,128]{2,1,0:T(8,128)(2,1)S(1)} %fusion.2), channel_id=1, source_target_pairs={{0,16},{8,24},{16,0},{24,8},{1,17},{9,25},{17,1},{25,9},{2,18},{10... | collective-permute-start | bytes 110600 | tf_op jit(solution)/shard_map/ppermute | solution.py:25
  50.4 4.0 %collective-permute-start.7 = (bf16[9,16,128]{2,1,0:T(8,128)(2,1)S(1)}, bf16[9,16,128]{2,1,0:T(8,128)(2,1)S(1)}, u32[]{:S(2)}, u32[]{:S(2)}) collective-permute-start(bf16[9,16,128]{2,1,0:T(8,128)(2,1)S(1)} %fusion.2), channel_id=1, source_target_pairs={{0,8},{8,0},{16,24},{24,16},{1,9},{9,1},{17,25},{25,17},{2,10},{10... | collective-permute-start | bytes 110600 | tf_op jit(solution)/shard_map/ppermute | solution.py:25
